TPU v7x, 32 devices: a whole 2x2x4 slice. The times are simulated.
32 devices in a mesh: row: 4 (over y, x), col: 8 (over z, core).
Axes of the slice: x: 2, y: 2, z: 4, core: 2. Of those that a mesh axis runs over, the one named last changes fastest.
Arguments:
- amplitudes: float32 [64, 64, 3072], P('row', None, 'col'), may hold values from -6 to 6
- integrals: float32 [3072, 800], P('col'), may hold values from -0.21875 to 0.21875
- occ_irrep: int32 [64], replicated, may hold values from 0 to 7, as said below
- cd_irrep: int32 [3072], P('col'), may hold values from 0 to 7, as said below
Outputs:
- residual: float32 [4096, 800], P(('row', 'col'))
Inputs may be any that keep to these rules, and one draw needn't show every extreme that they name: `occ_irrep`: D2h irrep labels; the orbitals are sorted by irrep: labels never fall along the orbitals, and every label occurs. `cd_irrep`: D2h irrep labels of the pairs; within each aligned block of 384 pairs the labels never fall and every label occurs.
All inputs are finite; a program needn't handle non-finite values.
Results may differ from a plain program's by a relative error of at most 0.0001.
Values sent between devices are 32-bit elements; how exact they have to be, the bound alone decides.
A program may use at most 64 MiB of HBM per device.

v0:
```python
import jax
import jax.numpy as jnp
from jax import lax
from jax.sharding import PartitionSpec as P


def body(amplitudes, integrals, occ_irrep, cd_irrep):
    own_count = amplitudes.shape[0]
    occupied = amplitudes.shape[1]
    received = lax.all_to_all(amplitudes, "row", split_axis=1, concat_axis=0, tiled=True)
    mirrored = jnp.swapaxes(received, 0, 1)
    first_i = lax.axis_index("row") * own_count
    own_irrep = lax.dynamic_slice_in_dim(occ_irrep, first_i, own_count, 0)
    pair_sym = jnp.bitwise_xor(own_irrep[:, None], occ_irrep[None, :])
    allowed = pair_sym[:, :, None] == cd_irrep[None, None, :]
    combined = jnp.where(allowed, amplitudes + mirrored, jnp.float32(0.0))
    combined = combined.reshape(own_count * occupied, amplitudes.shape[2])
    partial_value = jnp.dot(
        combined, integrals, precision=lax.Precision.HIGHEST, preferred_element_type=jnp.float32
    )
    return lax.psum_scatter(partial_value, "col", scatter_dimension=0, tiled=True)


def solution(mesh):
    in_specs = (P("row", None, "col"), P("col", None), P(), P("col"))
    out_specs = P(("row", "col"), None)
    return jax.shard_map(body, mesh=mesh, in_specs=in_specs, out_specs=out_specs, check_vma=False)
```

profile of v0, /device:TPU:0, one launch (start us, length us, event | category | flops | bytes accessed | tf_op | source)
XLA Modules:
  0.0 92.1 jit_solution(13736056444258499363)
XLA Ops:
  6.5 0.0 copy-start
  6.5 3.6 %copy.6 = f32[16,64,384]{2,0,1:T(8,128)} copy(f32[16,64,384]{2,1,0:T(8,128)} %param.4) | data formatting | bytes 3145728 | tf_op args[0]
  10.1 0.0 copy-start.3
  10.1 5.3 %all-to-all-start = ((f32[16,64,384]{2,0,1:T(8,128)}), f32[16,64,384]{2,0,1:T(8,128)S(1)}, u32[]{:S(2)}, u32[]{:S(2)}) async-start(f32[16,64,384]{2,0,1:T(8,128)} %copy.6), calls=%async_computation | async-start | bytes 3145728 | tf_op jit(solution)/shard_map/all_to_all | solution.py:10
  15.4 0.0 reduce-scatter.2.cloned.1.call-start
  15.4 0.0 copy-done.3
  15.4 0.1 dynamic_slice.3
  15.5 0.1 broadcast_xor_fusion
  15.6 19.1 %all-to-all-done = f32[16,64,384]{2,0,1:T(8,128)S(1)} async-done(((f32[16,64,384]{2,0,1:T(8,128)}), f32[16,64,384]{2,0,1:T(8,128)S(1)}, u32[]{:S(2)}, u32[]{:S(2)}) %all-to-all-start) | async-done | bytes 1572896 | tf_op jit(solution)/shard_map/all_to_all | solution.py:10
  34.7 0.0 copy-start.1
  34.7 0.0 copy-start.2
  34.7 0.2 copy.7
  34.8 1.2 %copy-done.1 = f32[16,64,384]{2,1,0:T(8,128)S(1)} copy-done((f32[16,64,384]{2,1,0:T(8,128)S(1)}, f32[16,64,384]{2,1,0:T(8,128)}, u32[]{:S(2)}) %copy-start.1) | copy-done | bytes 1572888
  36.1 0.0 copy-done.2
  36.1 0.3 fusion
  36.4 0.0 copy-done
  36.4 7.0 %fusion.1 = f32[1024,800]{0,1:T(8,128)} fusion(f32[1024,384]{1,0:T(8,128)S(1)} %bitcast.13, f32[384,800]{0,1:T(8,128)S(1)} %copy-done), kind=kOutput, calls=%fused_computation.3 | convolution fusion | flops 3774873600 | bytes 6078464 | tf_op jit(solution)/shard_map/dot_general | solution.py:18
  43.4 0.0 reduce-scatter.2.cloned.1.call-update
  43.4 41.9 %reduce-scatter.2.cloned.1.call-done = f32[128,800]{0,1:T(8,128)} async-done(((f32[1024,800]{0,1:T(8,128)}), f32[128,800]{0,1:T(8,128)}) %reduce-scatter.2.cloned.1.call-update) | async-done | bytes 409616 | tf_op jit(solution)/shard_map/reduce_scatter | solution.py:21
Async XLA Ops:
  6.5 29.8 %copy-start = (f32[384,800]{0,1:T(8,128)S(1)}, f32[384,800]{0,1:T(8,128)}, u32[]{:S(2)}) copy-start(f32[384,800]{0,1:T(8,128)} %param.5) | copy-start | bytes 3686404
  10.1 5.3 %copy-start.3 = (s32[64]{0:T(128)S(1)}, s32[64]{0:T(128)}, u32[]{:S(2)}) copy-start(s32[64]{0:T(128)} %param.6) | copy-start | bytes 772
  10.1 24.5 %all-to-all-start = ((f32[16,64,384]{2,0,1:T(8,128)}), f32[16,64,384]{2,0,1:T(8,128)S(1)}, u32[]{:S(2)}, u32[]{:S(2)}) async-start(f32[16,64,384]{2,0,1:T(8,128)} %copy.6), calls=%async_computation | async-start | bytes 3145728 | tf_op jit(solution)/shard_map/all_to_all | solution.py:10
  15.4 69.9 %reduce-scatter.2.cloned.1.call-start = ((), (), s32[]{:S(2)}) async-start(), calls=%async_computation.2 | async-start | bytes 3686400 | tf_op jit(solution)/shard_map/reduce_scatter | solution.py:21
  34.7 1.4 %copy-start.1 = (f32[16,64,384]{2,1,0:T(8,128)S(1)}, f32[16,64,384]{2,1,0:T(8,128)}, u32[]{:S(2)}) copy-start(f32[16,64,384]{2,1,0:T(8,128)} %param.4) | copy-start | bytes 4718596
  34.7 1.4 %copy-start.2 = (s32[384]{0:T(512)S(1)}, s32[384]{0:T(512)}, u32[]{:S(2)}) copy-start(s32[384]{0:T(512)} %param.7) | copy-start | bytes 4612
Sparse Core Ops, SparseCore 0:
  43.5 41.7 reduce-scatter.1
where the time goes:
time: 92.4 us; the launch traced here: 92.1 us
  waiting for transfers between devices  61 us (66%)
  between operations  13.4 us (15%)
  matrix products  7.02 us (8%)
  starting transfers between devices  5.3 us (6%)
  local copies, waits for them, and re-layouts  5.06 us (5%)
    reduce_scatter x1, waiting for transfers between devices, body(): lax.psum_scatter(partial_value, 'col', scatter_dimension=0, tiled=True)  41.9 us
    all_to_all x1, waiting for transfers between devices, body(): lax.all_to_all(amplitudes, 'row', split_axis=1, concat_axis=0, tiled=True)  19.1 us
    dot_general x1, matrix products, body(): jnp.dot(combined, integrals, precision=lax.Precision.HIGHEST, preferred_e...  7.02 us
    all_to_all x1, starting transfers between devices, body(): lax.all_to_all(amplitudes, 'row', split_axis=1, concat_axis=0, tiled=True)  5.29 us
    unnamed x9, local copies, waits for them, and re-layouts  4.82 us
  transfers between devices with their start and end apart: 2, of which 2 were waited for; matrix products, arithmetic and copies ran while one was open for 0% of the time, Pallas kernels for 0%

commit v1 on v0

--- a/solution.py
+++ b/solution.py
@@ -1,10 +1,15 @@
 import jax
 import jax.numpy as jnp
 from jax import lax
+from jax.experimental import pallas as pl
+from jax.experimental.pallas import tpu as pltpu
 from jax.sharding import PartitionSpec as P
 
-
-def body(amplitudes, integrals, occ_irrep, cd_irrep):
+MESH = pl.DeviceIdType.MESH
+BLOCKS = 9
+
+
+def plain_body(amplitudes, integrals, occ_irrep, cd_irrep):
     own_count = amplitudes.shape[0]
     occupied = amplitudes.shape[1]
     received = lax.all_to_all(amplitudes, "row", split_axis=1, concat_axis=0, tiled=True)
@@ -21,7 +26,338 @@
     return lax.psum_scatter(partial_value, "col", scatter_dimension=0, tiled=True)
 
 
+def split(value):
+    high = value.astype(jnp.bfloat16)
+    low = (value - high.astype(jnp.float32)).astype(jnp.bfloat16)
+    return high, low
+
+
+def kernel(
+    amp, vt, occ_s, occ_v, lab, out,
+    land, lhs, rhs, part, core_in, own, from_left, from_right, to_right, to_left,
+    final, sib, gsend, grecv, gsib,
+    a2a_s, a2a_r, loc, core_s, core_r, right_s, right_r, left_s, left_r, sib_s, sib_r, g_s, g_r, gs_s, gs_r,
+):
+    a, c = lax.axis_index("row"), lax.axis_index("col")
+    z, core = lax.div(c, 2), lax.rem(c, 2)
+    other = 1 - core
+    sibling = (a, 2 * z + other)
+    a_hi, a_lo = lax.div(a, 2), lax.rem(a, 2)
+    peers = [a, 2 * a_hi + 1 - a_lo, 2 * (1 - a_hi) + a_lo, 2 * (1 - a_hi) + 1 - a_lo]
+    flips = [None, a_lo, a_hi, a_hi]
+
+    def flip(h, s):
+        return s if h == 0 else 1 - s
+
+    def octet(index):
+        return pl.ds(pl.multiple_of(8 * index, 8), 8)
+
+    barrier = pltpu.get_barrier_semaphore()
+    pl.semaphore_signal(barrier, 1, device_id=sibling, device_id_type=MESH)
+    for t in (1, 2, 3):
+        pl.semaphore_signal(barrier, 1, device_id=(peers[t], c), device_id_type=MESH)
+
+    @pl.when(z > 0)
+    def _():
+        pl.semaphore_signal(barrier, 1, device_id=(a, c - 2), device_id_type=MESH)
+
+    @pl.when(z < 3)
+    def _():
+        pl.semaphore_signal(barrier, 1, device_id=(a, c + 2), device_id_type=MESH)
+
+    @pl.when((z == 0) | (z == 3))
+    def _():
+        pl.semaphore_wait(barrier, 5)
+
+    @pl.when((z == 1) | (z == 2))
+    def _():
+        pl.semaphore_wait(barrier, 6)
+
+    exchanged = {}
+    for t in (3, 1, 2):
+        for h in (0, 1):
+            n = 2 * (t - 1) + h
+            theirs = 1 - flips[t]
+            copy = pltpu.make_async_remote_copy(
+                src_ref=amp.at[octet(flip(h, theirs)), octet(2 * peers[t] + h), :],
+                dst_ref=land.at[n], send_sem=a2a_s.at[n], recv_sem=a2a_r.at[n],
+                device_id=(peers[t], c), device_id_type=MESH,
+            )
+            copy.start()
+            exchanged[n] = copy
+    local = {}
+    for n, (first, second) in ((6, (0, 0)), (7, (1, 1)), (8, (1, 0))):
+        copy = pltpu.make_async_copy(
+            amp.at[8 * first:8 * first + 8, octet(2 * a + second), :], land.at[n], loc.at[n - 6]
+        )
+        copy.start()
+        local[n] = copy
+
+    depth = vt.shape[1]
+    v_high, v_low = split(vt[...])
+    rhs[:, 0:depth] = v_high
+    rhs[:, depth:2 * depth] = v_low
+    rhs[:, 2 * depth:3 * depth] = v_high
+    labels = lab[...]
+
+    def block(n):
+        if n < 6:
+            t, h = n // 2 + 1, n % 2
+            exchanged[n].wait_recv()
+            own_oct, col = h, 2 * peers[t] + flip(h, flips[t])
+        else:
+            local[n].wait()
+            own_oct = 0 if n == 8 else n - 6
+            col = 2 * a + (1 if n == 8 else n - 6)
+        column_sym = occ_v[octet(col), :]
+        for i in range(8):
+            row = 8 * own_oct + i
+            pair_sym = jnp.bitwise_xor(column_sym, occ_s[16 * a + row])
+            total = amp[row, octet(col), :] + land[n, :, i, :]
+            total = jnp.where(pair_sym == labels, total, jnp.float32(0.0))
+            high, low = split(total)
+            lhs[8 * i:8 * i + 8, 0:depth] = high.astype(jnp.float32)
+            lhs[8 * i:8 * i + 8, depth:2 * depth] = low.astype(jnp.float32)
+        high = lhs[:, 0:depth].astype(jnp.bfloat16)
+        low = lhs[:, depth:2 * depth].astype(jnp.bfloat16)
+        stacked = jnp.concatenate([high, high, low], axis=1)
+        product = lax.dot_general(
+            stacked, rhs[...], (((1,), (1,)), ((), ())), preferred_element_type=jnp.float32
+        )
+        part[n] = product.reshape(8, 8, product.shape[1])
+        copy = pltpu.make_async_remote_copy(
+            src_ref=part.at[n, pl.ds(4 * other, 4)], dst_ref=core_in.at[n],
+            send_sem=core_s.at[n], recv_sem=core_r.at[n], device_id=sibling, device_id_type=MESH,
+        )
+        copy.start()
+        return copy
+
+    order = (6, 7, 8, 2, 3, 0, 1, 4, 5)
+
+    def chain(n, source, sems, target):
+        return pltpu.make_async_remote_copy(
+            src_ref=source.at[n], dst_ref=(from_left if sems == "right" else from_right).at[n],
+            send_sem=(right_s if sems == "right" else left_s).at[n],
+            recv_sem=(right_r if sems == "right" else left_r).at[n],
+            device_id=target, device_id_type=MESH,
+        )
+
+    def right(n, source):
+        return chain(n, source, "right", (a, lax.rem(c + 2, 8)))
+
+    def left(n, source):
+        return chain(n, source, "left", (a, lax.rem(c + 6, 8)))
+
+    core_copies = {}
+    previous = None
+
+    def gather(n):
+        core_copies[n].wait_recv()
+        own[n] = part[n, pl.ds(4 * core, 4)] + core_in[n]
+
+        @pl.when(z == 0)
+        def _():
+            right(n, own).start()
+
+        @pl.when(z == 3)
+        def _():
+            left(n, own).start()
+
+    for n in order:
+        core_copies[n] = block(n)
+        if previous is not None:
+            gather(previous)
+        previous = n
+    gather(previous)
+
+    def pass_right(n):
+        right(n, to_right).wait_recv()
+        to_right[n] = own[n] + from_left[n]
+        right(n, to_right).start()
+
+    def pass_left(n):
+        left(n, to_left).wait_recv()
+        to_left[n] = own[n] + from_right[n]
+        left(n, to_left).start()
+
+    lag = 2
+
+    @pl.when(z == 0)
+    def _():
+        for n in order:
+            left(n, own).wait_recv()
+            final[n] = own[n] + from_right[n]
+        for n in order:
+            right(n, own).wait_send()
+
+    @pl.when(z == 3)
+    def _():
+        for n in order:
+            right(n, own).wait_recv()
+            final[n] = own[n] + from_left[n]
+        for n in order:
+            left(n, own).wait_send()
+
+    @pl.when(z == 1)
+    def _():
+        for q in range(BLOCKS + lag):
+            if q < BLOCKS:
+                pass_right(order[q])
+            if q >= lag:
+                n = order[q - lag]
+                pass_left(n)
+                final[n] = to_right[n] + from_right[n]
+        for n in order:
+            right(n, to_right).wait_send()
+            left(n, to_left).wait_send()
+
+    @pl.when(z == 2)
+    def _():
+        for q in range(BLOCKS + lag):
+            if q < BLOCKS:
+                pass_left(order[q])
+            if q >= lag:
+                n = order[q - lag]
+                pass_right(n)
+                final[n] = to_left[n] + from_left[n]
+        for n in order:
+            right(n, to_right).wait_send()
+            left(n, to_left).wait_send()
+
+    half, odd = lax.div(z, 2), lax.rem(z, 2)
+    ends = []
+    g_copies = {}
+    for t in (3, 1, 2):
+        s = flips[t]
+        h = half + s - 2 * half * s
+        value = final[2 * (t - 1) + h]
+        for q in range(2):
+            rows = [
+                jnp.where(odd == 1, value[2 * q + e, 4:8, :], value[2 * q + e, 0:4, :]) for e in (0, 1)
+            ]
+            gsend[t - 1, q] = jnp.concatenate(rows, axis=0)
+        copy = pltpu.make_async_remote_copy(
+            src_ref=gsend.at[t - 1], dst_ref=grecv.at[t - 1], send_sem=g_s.at[t - 1],
+            recv_sem=g_r.at[t - 1], device_id=(peers[t], c), device_id_type=MESH,
+        )
+        copy.start()
+        g_copies[t] = copy
+    for slot in range(5):
+        index = (2 * slot + half) if slot < 4 else 8
+        copy = pltpu.make_async_remote_copy(
+            src_ref=final.at[index], dst_ref=sib.at[slot], send_sem=sib_s.at[slot],
+            recv_sem=sib_r.at[slot], device_id=sibling, device_id_type=MESH,
+        )
+        copy.start()
+        ends.append(copy)
+    for copy in ends:
+        copy.wait_recv()
+
+    def direct(slot, il):
+        mine = final[(2 * slot + half) if slot < 4 else 8, 2 * core + il]
+        theirs = sib[slot, 2 * core + il]
+        return jnp.where(odd == core, mine, theirs)
+
+    for il in range(2):
+        for t in (1, 2, 3):
+            s = flips[t]
+            out[il, octet(2 * peers[t] + (half + s - 2 * half * s)), :] = direct(t - 1, il)
+        out[il, octet(2 * a + half), :] = direct(3, il)
+        straight = direct(4, il)
+        rows = []
+        for j in range(8):
+            def pick(ref_row):
+                options = [ref_row[4 * o + 2 * k + il:4 * o + 2 * k + il + 1, :] for o in (0, 1) for k in (0, 1)]
+                even = jnp.where(core == 1, options[1], options[0])
+                uneven = jnp.where(core == 1, options[3], options[2])
+                return jnp.where(odd == 1, uneven, even)
+            mine, theirs = pick(final[8, j % 4]), pick(sib[4, j % 4])
+            rows.append(jnp.where(core == j // 4, mine, theirs))
+        turned = jnp.concatenate(rows, axis=0)
+        out[il, octet(2 * a + 1 - half), :] = jnp.where(half == 0, straight, turned)
+
+    g_sib = {}
+    for t in (3, 1, 2):
+        g_copies[t].wait_recv()
+        copy = pltpu.make_async_remote_copy(
+            src_ref=grecv.at[t - 1], dst_ref=gsib.at[t - 1], send_sem=gs_s.at[t - 1],
+            recv_sem=gs_r.at[t - 1], device_id=sibling, device_id_type=MESH,
+        )
+        copy.start()
+        g_sib[t] = copy
+    for t in (3, 1, 2):
+        g_sib[t].wait_recv()
+        s = flips[t]
+        g = 1 - (half + s - 2 * half * s)
+        for il in range(2):
+            rows = []
+            for j in range(8):
+                q, e = (j % 4) // 2, j % 2
+
+                def pick(tile):
+                    low = tile[4 * e + il:4 * e + il + 1, :]
+                    high = tile[4 * e + 2 + il:4 * e + 3 + il, :]
+                    return jnp.where(core == 1, high, low)
+                mine, theirs = pick(grecv[t - 1, q]), pick(gsib[t - 1, q])
+                rows.append(jnp.where(core == j // 4, mine, theirs))
+            out[il, octet(2 * peers[t] + g), :] = jnp.concatenate(rows, axis=0)
+
+    for n in range(6):
+        exchanged[n].wait_send()
+    for n in range(BLOCKS):
+        core_copies[n].wait_send()
+    for copy in ends:
+        copy.wait_send()
+    for t in (1, 2, 3):
+        g_copies[t].wait_send()
+        g_sib[t].wait_send()
+
+
+def paired_body(amplitudes, integrals, occ_irrep, cd_irrep):
+    depth, width = integrals.shape
+    vmem = pl.BlockSpec(memory_space=pltpu.VMEM)
+    smem = pl.BlockSpec(memory_space=pltpu.SMEM)
+    f32 = jnp.float32
+
+    def sums(count):
+        return pltpu.VMEM((count, 4, 8, width), f32)
+
+    def sems(count):
+        return [pltpu.SemaphoreType.DMA((count,))] * 2
+
+    result = pl.pallas_call(
+        kernel,
+        out_shape=jax.ShapeDtypeStruct((2, 64, width), f32),
+        in_specs=[vmem, vmem, smem, vmem, vmem],
+        out_specs=vmem,
+        scratch_shapes=[
+            pltpu.VMEM((BLOCKS, 8, 8, depth), f32),
+            pltpu.VMEM((64, 2 * depth), f32),
+            pltpu.VMEM((width, 3 * depth), jnp.bfloat16),
+            pltpu.VMEM((BLOCKS, 8, 8, width), f32),
+            sums(BLOCKS), sums(BLOCKS), sums(BLOCKS), sums(BLOCKS), sums(BLOCKS), sums(BLOCKS),
+            sums(BLOCKS), sums(5),
+            pltpu.VMEM((3, 2, 8, width), f32),
+            pltpu.VMEM((3, 2, 8, width), f32),
+            pltpu.VMEM((3, 2, 8, width), f32),
+            *sems(6), pltpu.SemaphoreType.DMA((3,)),
+            *sems(BLOCKS), *sems(BLOCKS), *sems(BLOCKS), *sems(5), *sems(3), *sems(3),
+        ],
+        compiler_params=pltpu.CompilerParams(
+            collective_id=0, has_side_effects=True, vmem_limit_bytes=50 << 20
+        ),
+    )(amplitudes, integrals.T, occ_irrep, occ_irrep.reshape(64, 1), cd_irrep.reshape(1, depth))
+    return result.reshape(128, width)
+
+
 def solution(mesh):
     in_specs = (P("row", None, "col"), P("col", None), P(), P("col"))
     out_specs = P(("row", "col"), None)
+    fits = mesh.shape["row"] == 4 and mesh.shape["col"] == 8
+
+    def body(amplitudes, integrals, occ_irrep, cd_irrep):
+        paired = fits and amplitudes.shape[:2] == (16, 64)
+        chosen = paired_body if paired else plain_body
+        return chosen(amplitudes, integrals, occ_irrep, cd_irrep)
+
     return jax.shard_map(body, mesh=mesh, in_specs=in_specs, out_specs=out_specs, check_vma=False)

time: 92.4 us -> 61.3 us (0.66)
  waiting for transfers between devices: 61 us -> 0 us
  Pallas kernels: 0 us -> 55.4 us
  between operations: 13.4 us -> 0.01 us
  matrix products: 7.02 us -> 0 us
  starting transfers between devices: 5.3 us -> 0 us
    pallas_call x0 -> x1, Pallas kernels: none -> 55.4 us  [paired_body(): pl.pallas_call(kernel, out_shape=jax.ShapeDtypeStruct((2, 64, width), f32...]
    reduce_scatter x1 -> x0, waiting for transfers between devices: 41.9 us -> none  [body(): lax.psum_scatter(partial_value, 'col', scatter_dimension=0, tiled=True)]
    all_to_all x1 -> x0, waiting for transfers between devices: 19.1 us -> none  [body(): lax.all_to_all(amplitudes, 'row', split_axis=1, concat_axis=0, tiled=True)]
    dot_general x1 -> x0, matrix products: 7.02 us -> none  [body(): jnp.dot(combined, integrals, precision=lax.Precision.HIGHEST, preferred_e...]
    all_to_all x1 -> x0, starting transfers between devices: 5.29 us -> none  [body(): lax.all_to_all(amplitudes, 'row', split_axis=1, concat_axis=0, tiled=True)]
    reshape x0 -> x3, local copies, waits for them, and re-layouts: none -> 2.35 us  [the longest x1 0.93 us: paired_body(): return result.reshape(128, width)]
    unnamed x9 -> x6, local copies, waits for them, and re-layouts: 4.82 us -> 3.35 us
  transfers between devices with their start and end apart: 2 -> 0, of which waited for: 2 -> 0; matrix products, arithmetic and copies ran while one was open for 0% -> 0% of each run, Pallas kernels for 0% -> 0%
where the time goes in v1:
time: 61.3 us; the launch traced here: 61.1 us
  Pallas kernels  55.4 us (90%)
  local copies, waits for them, and re-layouts  5.7 us (9%)
    pallas_call x1, Pallas kernels, paired_body(): pl.pallas_call(kernel, out_shape=jax.ShapeDtypeStruct((2, 64, width), f32...  55.4 us
    unnamed x6, local copies, waits for them, and re-layouts  3.35 us

profile of v1, /device:TPU:0, one launch (start us, length us, event | category | flops | bytes accessed | tf_op | source)
XLA Modules:
  0.0 61.1 jit_solution(10729259000442132941)
XLA Ops:
  0.0 0.7 %reshape.10.lab = s32[1,384]{1,0:T(1,128)S(1)} reshape(s32[384]{0:T(512)} %param.7) | data formatting | bytes 3072 | tf_op jit(solution)/shard_map/reshape | solution.py:349
  0.7 0.7 %copy.5.occ_v = s32[64,1]{1,0:T(8,128)S(1)} copy(s32[64,1]{0,1:T(1,128)} %bitcast.5) | data formatting | bytes 512 | tf_op jit(solution)/shard_map/reshape | solution.py:349
  1.4 0.0 copy-start
  1.4 1.4 %copy-done = f32[16,64,384]{2,1,0:T(8,128)S(1)} copy-done((f32[16,64,384]{2,1,0:T(8,128)S(1)}, f32[16,64,384]{2,1,0:T(8,128)}, u32[]{:S(2)}) %copy-start) | copy-done | bytes 1572888
  2.8 0.0 copy-start.1
  2.8 1.3 %copy-done.1 = f32[384,800]{0,1:T(8,128)S(1)} copy-done((f32[384,800]{0,1:T(8,128)S(1)}, f32[384,800]{0,1:T(8,128)}, u32[]{:S(2)}) %copy-start.1) | copy-done | bytes 1228824
  4.1 0.0 copy-start.2
  4.1 0.7 %copy-done.2 = s32[64]{0:T(128)S(1)} copy-done((s32[64]{0:T(128)S(1)}, s32[64]{0:T(128)}, u32[]{:S(2)}) %copy-start.2) | copy-done | bytes 280
  4.8 55.4 %shard_map.46 = f32[2,64,800]{2,1,0:T(8,128)S(1)} custom-call(f32[16,64,384]{2,1,0:T(8,128)S(1)} %copy-done, f32[800,384]{1,0:T(8,128)S(1)} %bitcast.4, s32[64]{0:T(128)S(1)} %copy-done.2, s32[64,1]{1,0:T(8,128)S(1)} %copy.5.occ_v, s32[1,384]{1,0:T(1,128)S(1)} %reshape.10.lab), custom_call_target="tpu_custom_call" | custom-call | tf_op jit(solution)/shard_map/pallas_call | solution.py:328
  60.2 0.9 %copy.6 = f32[128,800]{0,1:T(8,128)} copy(f32[128,800]{1,0:T(8,128)S(1)} %bitcast.3) | data formatting | bytes 819200 | tf_op jit(solution)/shard_map/reshape | solution.py:350
Async XLA Ops:
  1.4 1.4 %copy-start = (f32[16,64,384]{2,1,0:T(8,128)S(1)}, f32[16,64,384]{2,1,0:T(8,128)}, u32[]{:S(2)}) copy-start(f32[16,64,384]{2,1,0:T(8,128)} %amp.1) | copy-start | bytes 4718596
  2.8 1.3 %copy-start.1 = (f32[384,800]{0,1:T(8,128)S(1)}, f32[384,800]{0,1:T(8,128)}, u32[]{:S(2)}) copy-start(f32[384,800]{0,1:T(8,128)} %param.5) | copy-start | bytes 3686404
  4.1 0.7 %copy-start.2 = (s32[64]{0:T(128)S(1)}, s32[64]{0:T(128)}, u32[]{:S(2)}) copy-start(s32[64]{0:T(128)} %occ_s.1) | copy-start | bytes 772

commit v2 on v1

--- a/solution.py
+++ b/solution.py
@@ -99,8 +99,9 @@
     rhs[:, depth:2 * depth] = v_low
     rhs[:, 2 * depth:3 * depth] = v_high
     labels = lab[...]
-
-    def block(n):
+    core_copies = {}
+
+    def fill(n, base):
         if n < 6:
             t, h = n // 2 + 1, n % 2
             exchanged[n].wait_recv()
@@ -116,23 +117,30 @@
             total = amp[row, octet(col), :] + land[n, :, i, :]
             total = jnp.where(pair_sym == labels, total, jnp.float32(0.0))
             high, low = split(total)
-            lhs[8 * i:8 * i + 8, 0:depth] = high.astype(jnp.float32)
-            lhs[8 * i:8 * i + 8, depth:2 * depth] = low.astype(jnp.float32)
-        high = lhs[:, 0:depth].astype(jnp.bfloat16)
-        low = lhs[:, depth:2 * depth].astype(jnp.bfloat16)
+            lhs[base + 8 * i:base + 8 * i + 8, 0:depth] = high.astype(jnp.float32)
+            lhs[base + 8 * i:base + 8 * i + 8, depth:2 * depth] = low.astype(jnp.float32)
+
+    def multiply(group):
+        rows = 64 * len(group)
+        for slot, n in enumerate(group):
+            fill(n, 64 * slot)
+        high = lhs[0:rows, 0:depth].astype(jnp.bfloat16)
+        low = lhs[0:rows, depth:2 * depth].astype(jnp.bfloat16)
         stacked = jnp.concatenate([high, high, low], axis=1)
         product = lax.dot_general(
             stacked, rhs[...], (((1,), (1,)), ((), ())), preferred_element_type=jnp.float32
         )
-        part[n] = product.reshape(8, 8, product.shape[1])
-        copy = pltpu.make_async_remote_copy(
-            src_ref=part.at[n, pl.ds(4 * other, 4)], dst_ref=core_in.at[n],
-            send_sem=core_s.at[n], recv_sem=core_r.at[n], device_id=sibling, device_id_type=MESH,
-        )
-        copy.start()
-        return copy
-
-    order = (6, 7, 8, 2, 3, 0, 1, 4, 5)
+        for slot, n in enumerate(group):
+            part[n] = product[64 * slot:64 * slot + 64].reshape(8, 8, product.shape[1])
+            copy = pltpu.make_async_remote_copy(
+                src_ref=part.at[n, pl.ds(4 * other, 4)], dst_ref=core_in.at[n],
+                send_sem=core_s.at[n], recv_sem=core_r.at[n], device_id=sibling, device_id_type=MESH,
+            )
+            copy.start()
+            core_copies[n] = copy
+
+    groups = ((6, 7, 8), (4, 5, 0, 1), (2, 3))
+    order = sum(groups, ())
 
     def chain(n, source, sems, target):
         return pltpu.make_async_remote_copy(
@@ -148,9 +156,6 @@
     def left(n, source):
         return chain(n, source, "left", (a, lax.rem(c + 6, 8)))
 
-    core_copies = {}
-    previous = None
-
     def gather(n):
         core_copies[n].wait_recv()
         own[n] = part[n, pl.ds(4 * core, 4)] + core_in[n]
@@ -163,12 +168,10 @@
         def _():
             left(n, own).start()
 
-    for n in order:
-        core_copies[n] = block(n)
-        if previous is not None:
-            gather(previous)
-        previous = n
-    gather(previous)
+    for group in groups:
+        multiply(group)
+        for n in group:
+            gather(n)
 
     def pass_right(n):
         right(n, to_right).wait_recv()
@@ -332,7 +335,7 @@
         out_specs=vmem,
         scratch_shapes=[
             pltpu.VMEM((BLOCKS, 8, 8, depth), f32),
-            pltpu.VMEM((64, 2 * depth), f32),
+            pltpu.VMEM((256, 2 * depth), f32),
             pltpu.VMEM((width, 3 * depth), jnp.bfloat16),
             pltpu.VMEM((BLOCKS, 8, 8, width), f32),
             sums(BLOCKS), sums(BLOCKS), sums(BLOCKS), sums(BLOCKS), sums(BLOCKS), sums(BLOCKS),

time: 61.3 us -> 59 us (0.962)
  Pallas kernels: 55.4 us -> 53.1 us
    pallas_call x1, Pallas kernels: 55.4 us -> 53.1 us  [paired_body(): pl.pallas_call(kernel, out_shape=jax.ShapeDtypeStruct((2, 64, width), f32...]
where the time goes in v2:
time: 59 us; the launch traced here: 58.8 us
  Pallas kernels  53.1 us (90%)
  local copies, waits for them, and re-layouts  5.7 us (10%)
    pallas_call x1, Pallas kernels, paired_body(): pl.pallas_call(kernel, out_shape=jax.ShapeDtypeStruct((2, 64, width), f32...  53.1 us
    unnamed x6, local copies, waits for them, and re-layouts  3.35 us

profile of v2, /device:TPU:0, one launch (start us, length us, event | category | flops | bytes accessed | tf_op | source)
XLA Modules:
  0.0 58.8 jit_solution(13609280841598641542)
XLA Ops:
  0.0 0.7 %reshape.10.lab = s32[1,384]{1,0:T(1,128)S(1)} reshape(s32[384]{0:T(512)} %param.7) | data formatting | bytes 3072 | tf_op jit(solution)/shard_map/reshape | solution.py:352
  0.7 0.7 %copy.5.occ_v = s32[64,1]{1,0:T(8,128)S(1)} copy(s32[64,1]{0,1:T(1,128)} %bitcast.5) | data formatting | bytes 512 | tf_op jit(solution)/shard_map/reshape | solution.py:352
  1.4 0.0 copy-start
  1.4 1.4 %copy-done = f32[16,64,384]{2,1,0:T(8,128)S(1)} copy-done((f32[16,64,384]{2,1,0:T(8,128)S(1)}, f32[16,64,384]{2,1,0:T(8,128)}, u32[]{:S(2)}) %copy-start) | copy-done | bytes 1572888
  2.8 0.0 copy-start.1
  2.8 1.3 %copy-done.1 = f32[384,800]{0,1:T(8,128)S(1)} copy-done((f32[384,800]{0,1:T(8,128)S(1)}, f32[384,800]{0,1:T(8,128)}, u32[]{:S(2)}) %copy-start.1) | copy-done | bytes 1228824
  4.1 0.0 copy-start.2
  4.1 0.7 %copy-done.2 = s32[64]{0:T(128)S(1)} copy-done((s32[64]{0:T(128)S(1)}, s32[64]{0:T(128)}, u32[]{:S(2)}) %copy-start.2) | copy-done | bytes 280
  4.8 53.1 %shard_map.46 = f32[2,64,800]{2,1,0:T(8,128)S(1)} custom-call(f32[16,64,384]{2,1,0:T(8,128)S(1)} %copy-done, f32[800,384]{1,0:T(8,128)S(1)} %bitcast.4, s32[64]{0:T(128)S(1)} %copy-done.2, s32[64,1]{1,0:T(8,128)S(1)} %copy.5.occ_v, s32[1,384]{1,0:T(1,128)S(1)} %reshape.10.lab), custom_call_target="tpu_custom_call" | custom-call | tf_op jit(solution)/shard_map/pallas_call | solution.py:331
  57.8 0.9 %copy.6 = f32[128,800]{0,1:T(8,128)} copy(f32[128,800]{1,0:T(8,128)S(1)} %bitcast.3) | data formatting | bytes 819200 | tf_op jit(solution)/shard_map/reshape | solution.py:353
Async XLA Ops:
  1.4 1.4 %copy-start = (f32[16,64,384]{2,1,0:T(8,128)S(1)}, f32[16,64,384]{2,1,0:T(8,128)}, u32[]{:S(2)}) copy-start(f32[16,64,384]{2,1,0:T(8,128)} %amp.1) | copy-start | bytes 4718596
  2.8 1.3 %copy-start.1 = (f32[384,800]{0,1:T(8,128)S(1)}, f32[384,800]{0,1:T(8,128)}, u32[]{:S(2)}) copy-start(f32[384,800]{0,1:T(8,128)} %param.5) | copy-start | bytes 3686404
  4.1 0.7 %copy-start.2 = (s32[64]{0:T(128)S(1)}, s32[64]{0:T(128)}, u32[]{:S(2)}) copy-start(s32[64]{0:T(128)} %occ_s.1) | copy-start | bytes 772

commit v3 on v2

--- a/solution.py
+++ b/solution.py
@@ -33,8 +33,8 @@
 
 
 def kernel(
-    amp, vt, occ_s, occ_v, lab, out,
-    land, lhs, rhs, part, core_in, own, from_left, from_right, to_right, to_left,
+    amp_hbm, vt_hbm, occ_s, lab, out,
+    amp, vt, in_sem, land, lhs, rhs, part, core_in, own, from_left, from_right, to_right, to_left,
     final, sib, gsend, grecv, gsib,
     a2a_s, a2a_r, loc, core_s, core_r, right_s, right_r, left_s, left_r, sib_s, sib_r, g_s, g_r, gs_s, gs_r,
 ):
@@ -52,6 +52,10 @@
     def octet(index):
         return pl.ds(pl.multiple_of(8 * index, 8), 8)
 
+    amp_copy = pltpu.make_async_copy(amp_hbm, amp, in_sem.at[0])
+    vt_copy = pltpu.make_async_copy(vt_hbm, vt, in_sem.at[1])
+    vt_copy.start()
+    amp_copy.start()
     barrier = pltpu.get_barrier_semaphore()
     pl.semaphore_signal(barrier, 1, device_id=sibling, device_id_type=MESH)
     for t in (1, 2, 3):
@@ -79,7 +83,7 @@
             n = 2 * (t - 1) + h
             theirs = 1 - flips[t]
             copy = pltpu.make_async_remote_copy(
-                src_ref=amp.at[octet(flip(h, theirs)), octet(2 * peers[t] + h), :],
+                src_ref=amp_hbm.at[octet(flip(h, theirs)), octet(2 * peers[t] + h), :],
                 dst_ref=land.at[n], send_sem=a2a_s.at[n], recv_sem=a2a_r.at[n],
                 device_id=(peers[t], c), device_id_type=MESH,
             )
@@ -88,17 +92,28 @@
     local = {}
     for n, (first, second) in ((6, (0, 0)), (7, (1, 1)), (8, (1, 0))):
         copy = pltpu.make_async_copy(
-            amp.at[8 * first:8 * first + 8, octet(2 * a + second), :], land.at[n], loc.at[n - 6]
+            amp_hbm.at[8 * first:8 * first + 8, octet(2 * a + second), :], land.at[n], loc.at[n - 6]
         )
         copy.start()
         local[n] = copy
 
-    depth = vt.shape[1]
+    width, depth = vt.shape
+    full = width // 128
+    rest = width % 128
+
+    def unpack(packed, i):
+        tiles = [packed[full * i + lane] for lane in range(full)]
+        return jnp.concatenate(tiles + [packed[4 * full][:, rest * i:rest * i + rest]], axis=1)
+
+    half, odd = lax.div(z, 2), lax.rem(z, 2)
+    vt_copy.wait()
     v_high, v_low = split(vt[...])
     rhs[:, 0:depth] = v_high
     rhs[:, depth:2 * depth] = v_low
     rhs[:, 2 * depth:3 * depth] = v_high
-    labels = lab[...]
+    amp_copy.wait()
+    labels = lab[...].reshape(1, depth)
+    sublane = lax.broadcasted_iota(jnp.int32, (8, depth), 0)
     core_copies = {}
 
     def fill(n, base):
@@ -110,12 +125,14 @@
             local[n].wait()
             own_oct = 0 if n == 8 else n - 6
             col = 2 * a + (1 if n == 8 else n - 6)
-        column_sym = occ_v[octet(col), :]
+        column_sym = jnp.zeros((8, depth), jnp.int32)
+        for j in range(8):
+            column_sym = jnp.where(sublane == j, occ_s[8 * col + j], column_sym)
+        column_sym = jnp.bitwise_xor(column_sym, labels)
         for i in range(8):
             row = 8 * own_oct + i
-            pair_sym = jnp.bitwise_xor(column_sym, occ_s[16 * a + row])
             total = amp[row, octet(col), :] + land[n, :, i, :]
-            total = jnp.where(pair_sym == labels, total, jnp.float32(0.0))
+            total = jnp.where(column_sym == occ_s[16 * a + row], total, jnp.float32(0.0))
             high, low = split(total)
             lhs[base + 8 * i:base + 8 * i + 8, 0:depth] = high.astype(jnp.float32)
             lhs[base + 8 * i:base + 8 * i + 8, depth:2 * depth] = low.astype(jnp.float32)
@@ -131,9 +148,14 @@
             stacked, rhs[...], (((1,), (1,)), ((), ())), preferred_element_type=jnp.float32
         )
         for slot, n in enumerate(group):
-            part[n] = product[64 * slot:64 * slot + 64].reshape(8, 8, product.shape[1])
+            for k in range(2):
+                rows_of = [product[64 * slot + 32 * k + 8 * i:64 * slot + 32 * k + 8 * i + 8] for i in range(4)]
+                for i in range(4):
+                    for lane in range(full):
+                        part[n, k, full * i + lane] = rows_of[i][:, 128 * lane:128 * lane + 128]
+                part[n, k, 4 * full] = jnp.concatenate([r[:, 128 * full:] for r in rows_of], axis=1)
             copy = pltpu.make_async_remote_copy(
-                src_ref=part.at[n, pl.ds(4 * other, 4)], dst_ref=core_in.at[n],
+                src_ref=part.at[n, other], dst_ref=core_in.at[n],
                 send_sem=core_s.at[n], recv_sem=core_r.at[n], device_id=sibling, device_id_type=MESH,
             )
             copy.start()
@@ -158,7 +180,7 @@
 
     def gather(n):
         core_copies[n].wait_recv()
-        own[n] = part[n, pl.ds(4 * core, 4)] + core_in[n]
+        own[n] = part[n, core] + core_in[n]
 
         @pl.when(z == 0)
         def _():
@@ -173,6 +195,31 @@
         for n in group:
             gather(n)
 
+    def g_copy(t):
+        return pltpu.make_async_remote_copy(
+            src_ref=gsend.at[t - 1], dst_ref=grecv.at[t - 1], send_sem=g_s.at[t - 1],
+            recv_sem=g_r.at[t - 1], device_id=(peers[t], c), device_id_type=MESH,
+        )
+
+    def sib_copy(slot):
+        return pltpu.make_async_remote_copy(
+            src_ref=final.at[(2 * slot + half) if slot < 4 else 8], dst_ref=sib.at[slot],
+            send_sem=sib_s.at[slot], recv_sem=sib_r.at[slot], device_id=sibling, device_id_type=MESH,
+        )
+
+    def finish(n):
+        if n in (1, 3, 5):
+            t = n // 2 + 1
+            s = flips[t]
+            value = final[2 * (t - 1) + (half + s - 2 * half * s)]
+            for q in range(2):
+                pair = [unpack(value, 2 * q + e) for e in (0, 1)]
+                rows = [jnp.where(odd == 1, p[4:8, :], p[0:4, :]) for p in pair]
+                gsend[t - 1, q] = jnp.concatenate(rows, axis=0)
+            g_copy(t).start()
+        if n in (1, 3, 5, 7, 8):
+            sib_copy(n // 2).start()
+
     def pass_right(n):
         right(n, to_right).wait_recv()
         to_right[n] = own[n] + from_left[n]
@@ -190,6 +237,7 @@
         for n in order:
             left(n, own).wait_recv()
             final[n] = own[n] + from_right[n]
+            finish(n)
         for n in order:
             right(n, own).wait_send()
 
@@ -198,6 +246,7 @@
         for n in order:
             right(n, own).wait_recv()
             final[n] = own[n] + from_left[n]
+            finish(n)
         for n in order:
             left(n, own).wait_send()
 
@@ -210,6 +259,7 @@
                 n = order[q - lag]
                 pass_left(n)
                 final[n] = to_right[n] + from_right[n]
+                finish(n)
         for n in order:
             right(n, to_right).wait_send()
             left(n, to_left).wait_send()
@@ -223,43 +273,20 @@
                 n = order[q - lag]
                 pass_right(n)
                 final[n] = to_left[n] + from_left[n]
+                finish(n)
         for n in order:
             right(n, to_right).wait_send()
             left(n, to_left).wait_send()
 
-    half, odd = lax.div(z, 2), lax.rem(z, 2)
-    ends = []
-    g_copies = {}
-    for t in (3, 1, 2):
-        s = flips[t]
-        h = half + s - 2 * half * s
-        value = final[2 * (t - 1) + h]
-        for q in range(2):
-            rows = [
-                jnp.where(odd == 1, value[2 * q + e, 4:8, :], value[2 * q + e, 0:4, :]) for e in (0, 1)
-            ]
-            gsend[t - 1, q] = jnp.concatenate(rows, axis=0)
-        copy = pltpu.make_async_remote_copy(
-            src_ref=gsend.at[t - 1], dst_ref=grecv.at[t - 1], send_sem=g_s.at[t - 1],
-            recv_sem=g_r.at[t - 1], device_id=(peers[t], c), device_id_type=MESH,
-        )
-        copy.start()
-        g_copies[t] = copy
-    for slot in range(5):
-        index = (2 * slot + half) if slot < 4 else 8
-        copy = pltpu.make_async_remote_copy(
-            src_ref=final.at[index], dst_ref=sib.at[slot], send_sem=sib_s.at[slot],
-            recv_sem=sib_r.at[slot], device_id=sibling, device_id_type=MESH,
-        )
-        copy.start()
-        ends.append(copy)
+    g_copies = {t: g_copy(t) for t in (3, 1, 2)}
+    ends = [sib_copy(slot) for slot in range(5)]
     for copy in ends:
         copy.wait_recv()
 
     def direct(slot, il):
-        mine = final[(2 * slot + half) if slot < 4 else 8, 2 * core + il]
-        theirs = sib[slot, 2 * core + il]
-        return jnp.where(odd == core, mine, theirs)
+        mine = final[(2 * slot + half) if slot < 4 else 8]
+        chosen = jnp.where(odd == core, mine, sib[slot])
+        return jnp.where(core == 1, unpack(chosen, 2 + il), unpack(chosen, il))
 
     for il in range(2):
         for t in (1, 2, 3):
@@ -268,13 +295,14 @@
         out[il, octet(2 * a + half), :] = direct(3, il)
         straight = direct(4, il)
         rows = []
+        mine_all, theirs_all = final[8], sib[4]
         for j in range(8):
             def pick(ref_row):
                 options = [ref_row[4 * o + 2 * k + il:4 * o + 2 * k + il + 1, :] for o in (0, 1) for k in (0, 1)]
                 even = jnp.where(core == 1, options[1], options[0])
                 uneven = jnp.where(core == 1, options[3], options[2])
                 return jnp.where(odd == 1, uneven, even)
-            mine, theirs = pick(final[8, j % 4]), pick(sib[4, j % 4])
+            mine, theirs = pick(unpack(mine_all, j % 4)), pick(unpack(theirs_all, j % 4))
             rows.append(jnp.where(core == j // 4, mine, theirs))
         turned = jnp.concatenate(rows, axis=0)
         out[il, octet(2 * a + 1 - half), :] = jnp.where(half == 0, straight, turned)
@@ -319,11 +347,13 @@
 def paired_body(amplitudes, integrals, occ_irrep, cd_irrep):
     depth, width = integrals.shape
     vmem = pl.BlockSpec(memory_space=pltpu.VMEM)
+    hbm = pl.BlockSpec(memory_space=pl.ANY)
     smem = pl.BlockSpec(memory_space=pltpu.SMEM)
     f32 = jnp.float32
+    tiles = 4 * (width // 128) + 1
 
     def sums(count):
-        return pltpu.VMEM((count, 4, 8, width), f32)
+        return pltpu.VMEM((count, tiles, 8, 128), f32)
 
     def sems(count):
         return [pltpu.SemaphoreType.DMA((count,))] * 2
@@ -331,13 +361,16 @@
     result = pl.pallas_call(
         kernel,
         out_shape=jax.ShapeDtypeStruct((2, 64, width), f32),
-        in_specs=[vmem, vmem, smem, vmem, vmem],
+        in_specs=[hbm, hbm, smem, vmem],
         out_specs=vmem,
         scratch_shapes=[
+            pltpu.VMEM(amplitudes.shape, f32),
+            pltpu.VMEM((width, depth), f32),
+            pltpu.SemaphoreType.DMA((2,)),
             pltpu.VMEM((BLOCKS, 8, 8, depth), f32),
             pltpu.VMEM((256, 2 * depth), f32),
             pltpu.VMEM((width, 3 * depth), jnp.bfloat16),
-            pltpu.VMEM((BLOCKS, 8, 8, width), f32),
+            pltpu.VMEM((BLOCKS, 2, tiles, 8, 128), f32),
             sums(BLOCKS), sums(BLOCKS), sums(BLOCKS), sums(BLOCKS), sums(BLOCKS), sums(BLOCKS),
             sums(BLOCKS), sums(5),
             pltpu.VMEM((3, 2, 8, width), f32),
@@ -349,7 +382,7 @@
         compiler_params=pltpu.CompilerParams(
             collective_id=0, has_side_effects=True, vmem_limit_bytes=50 << 20
         ),
-    )(amplitudes, integrals.T, occ_irrep, occ_irrep.reshape(64, 1), cd_irrep.reshape(1, depth))
+    )(amplitudes, integrals.T, occ_irrep, cd_irrep)
     return result.reshape(128, width)
 
 
@@ -359,7 +392,7 @@
     fits = mesh.shape["row"] == 4 and mesh.shape["col"] == 8
 
     def body(amplitudes, integrals, occ_irrep, cd_irrep):
-        paired = fits and amplitudes.shape[:2] == (16, 64)
+        paired = fits and amplitudes.shape[:2] == (16, 64) and integrals.shape[1] % 128 == 32
         chosen = paired_body if paired else plain_body
         return chosen(amplitudes, integrals, occ_irrep, cd_irrep)
 

time: 59 us -> 55.6 us (0.942)
  Pallas kernels: 53.1 us -> 50.5 us
  local copies, waits for them, and re-layouts: 5.7 us -> 4.96 us
    pallas_call x1, Pallas kernels: 53.1 us -> 50.5 us  [paired_body(): pl.pallas_call(kernel, out_shape=jax.ShapeDtypeStruct((2, 64, width), f32...]
    reshape x2 -> x0, local copies, waits for them, and re-layouts: 1.43 us -> none  [the longest x1 0.74 us: paired_body(): occ_irrep.reshape(64, 1)]
    unnamed x6 -> x8, local copies, waits for them, and re-layouts: 3.35 us -> 4.03 us
where the time goes in v3:
time: 55.6 us; the launch traced here: 55.4 us
  Pallas kernels  50.5 us (91%)
  local copies, waits for them, and re-layouts  4.96 us (9%)
    pallas_call x1, Pallas kernels, paired_body(): pl.pallas_call(kernel, out_shape=jax.ShapeDtypeStruct((2, 64, width), f32...  50.5 us
    unnamed x8, local copies, waits for them, and re-layouts  4.03 us

profile of v3, /device:TPU:0, one launch (start us, length us, event | category | flops | bytes accessed | tf_op | source)
XLA Modules:
  0.0 55.4 jit_solution(3921125762211511737)
XLA Ops:
  0.0 0.0 copy-start
  0.0 1.4 %copy-done = f32[16,64,384]{2,1,0:T(8,128)S(1)} copy-done((f32[16,64,384]{2,1,0:T(8,128)S(1)}, f32[16,64,384]{2,1,0:T(8,128)}, u32[]{:S(2)}) %copy-start) | copy-done | bytes 1572888
  1.4 0.0 copy-start.1
  1.4 1.3 %copy-done.1 = f32[384,800]{0,1:T(8,128)S(1)} copy-done((f32[384,800]{0,1:T(8,128)S(1)}, f32[384,800]{0,1:T(8,128)}, u32[]{:S(2)}) %copy-start.1) | copy-done | bytes 1228824
  2.7 0.0 copy-start.2
  2.7 0.7 %copy-done.2 = s32[384]{0:T(512)S(1)} copy-done((s32[384]{0:T(512)S(1)}, s32[384]{0:T(512)}, u32[]{:S(2)}) %copy-start.2) | copy-done | bytes 1560
  3.4 0.0 copy-start.3
  3.4 0.7 %copy-done.3 = s32[64]{0:T(128)S(1)} copy-done((s32[64]{0:T(128)S(1)}, s32[64]{0:T(128)}, u32[]{:S(2)}) %copy-start.3) | copy-done | bytes 280
  4.0 50.5 %shard_map.46 = f32[2,64,800]{2,1,0:T(8,128)S(1)} custom-call(f32[16,64,384]{2,1,0:T(8,128)S(1)} %copy-done, f32[800,384]{1,0:T(8,128)S(1)} %bitcast.3, s32[64]{0:T(128)S(1)} %copy-done.3, s32[384]{0:T(512)S(1)} %copy-done.2), custom_call_target="tpu_custom_call" | custom-call | tf_op jit(solution)/shard_map/pallas_call | solution.py:361
  54.5 0.9 %copy.5 = f32[128,800]{0,1:T(8,128)} copy(f32[128,800]{1,0:T(8,128)S(1)} %bitcast.2) | data formatting | bytes 819200 | tf_op jit(solution)/shard_map/reshape | solution.py:386
Async XLA Ops:
  0.0 1.4 %copy-start = (f32[16,64,384]{2,1,0:T(8,128)S(1)}, f32[16,64,384]{2,1,0:T(8,128)}, u32[]{:S(2)}) copy-start(f32[16,64,384]{2,1,0:T(8,128)} %amp_hbm.1) | copy-start | bytes 4718596
  1.4 1.3 %copy-start.1 = (f32[384,800]{0,1:T(8,128)S(1)}, f32[384,800]{0,1:T(8,128)}, u32[]{:S(2)}) copy-start(f32[384,800]{0,1:T(8,128)} %param.5) | copy-start | bytes 3686404
  2.7 0.7 %copy-start.2 = (s32[384]{0:T(512)S(1)}, s32[384]{0:T(512)}, u32[]{:S(2)}) copy-start(s32[384]{0:T(512)} %lab.1) | copy-start | bytes 4612
  3.4 0.7 %copy-start.3 = (s32[64]{0:T(128)S(1)}, s32[64]{0:T(128)}, u32[]{:S(2)}) copy-start(s32[64]{0:T(128)} %occ_s.1) | copy-start | bytes 772

commit v4 on v3

--- a/solution.py
+++ b/solution.py
@@ -161,7 +161,7 @@
             copy.start()
             core_copies[n] = copy
 
-    groups = ((6, 7, 8), (4, 5, 0, 1), (2, 3))
+    groups = ((6, 7, 8), (4, 5), (0, 1), (2, 3))
     order = sum(groups, ())
 
     def chain(n, source, sems, target):

time: 55.6 us -> 55.3 us (level)
  no operation moved by 1% of the time
where the time goes in v4:
time: 55.3 us; the launch traced here: 55.1 us
  Pallas kernels  50.1 us (91%)
  local copies, waits for them, and re-layouts  4.96 us (9%)
    pallas_call x1, Pallas kernels, paired_body(): pl.pallas_call(kernel, out_shape=jax.ShapeDtypeStruct((2, 64, width), f32...  50.1 us
    unnamed x8, local copies, waits for them, and re-layouts  4.03 us

profile of v4, /device:TPU:0, one launch (start us, length us, event | category | flops | bytes accessed | tf_op | source)
XLA Modules:
  0.0 55.1 jit_solution(9912860390541486877)
XLA Ops:
  0.0 0.0 copy-start
  0.0 1.4 %copy-done = f32[16,64,384]{2,1,0:T(8,128)S(1)} copy-done((f32[16,64,384]{2,1,0:T(8,128)S(1)}, f32[16,64,384]{2,1,0:T(8,128)}, u32[]{:S(2)}) %copy-start) | copy-done | bytes 1572888
  1.4 0.0 copy-start.1
  1.4 1.3 %copy-done.1 = f32[384,800]{0,1:T(8,128)S(1)} copy-done((f32[384,800]{0,1:T(8,128)S(1)}, f32[384,800]{0,1:T(8,128)}, u32[]{:S(2)}) %copy-start.1) | copy-done | bytes 1228824
  2.7 0.0 copy-start.2
  2.7 0.7 %copy-done.2 = s32[384]{0:T(512)S(1)} copy-done((s32[384]{0:T(512)S(1)}, s32[384]{0:T(512)}, u32[]{:S(2)}) %copy-start.2) | copy-done | bytes 1560
  3.4 0.0 copy-start.3
  3.4 0.7 %copy-done.3 = s32[64]{0:T(128)S(1)} copy-done((s32[64]{0:T(128)S(1)}, s32[64]{0:T(128)}, u32[]{:S(2)}) %copy-start.3) | copy-done | bytes 280
  4.0 50.1 %shard_map.46 = f32[2,64,800]{2,1,0:T(8,128)S(1)} custom-call(f32[16,64,384]{2,1,0:T(8,128)S(1)} %copy-done, f32[800,384]{1,0:T(8,128)S(1)} %bitcast.3, s32[64]{0:T(128)S(1)} %copy-done.3, s32[384]{0:T(512)S(1)} %copy-done.2), custom_call_target="tpu_custom_call" | custom-call | tf_op jit(solution)/shard_map/pallas_call | solution.py:361
  54.1 0.9 %copy.5 = f32[128,800]{0,1:T(8,128)} copy(f32[128,800]{1,0:T(8,128)S(1)} %bitcast.2) | data formatting | bytes 819200 | tf_op jit(solution)/shard_map/reshape | solution.py:386
Async XLA Ops:
  0.0 1.4 %copy-start = (f32[16,64,384]{2,1,0:T(8,128)S(1)}, f32[16,64,384]{2,1,0:T(8,128)}, u32[]{:S(2)}) copy-start(f32[16,64,384]{2,1,0:T(8,128)} %amp_hbm.1) | copy-start | bytes 4718596
  1.4 1.3 %copy-start.1 = (f32[384,800]{0,1:T(8,128)S(1)}, f32[384,800]{0,1:T(8,128)}, u32[]{:S(2)}) copy-start(f32[384,800]{0,1:T(8,128)} %param.5) | copy-start | bytes 3686404
  2.7 0.7 %copy-start.2 = (s32[384]{0:T(512)S(1)}, s32[384]{0:T(512)}, u32[]{:S(2)}) copy-start(s32[384]{0:T(512)} %lab.1) | copy-start | bytes 4612
  3.4 0.7 %copy-start.3 = (s32[64]{0:T(128)S(1)}, s32[64]{0:T(128)}, u32[]{:S(2)}) copy-start(s32[64]{0:T(128)} %occ_s.1) | copy-start | bytes 772
